TPU v7x, 32 devices: a whole 2x2x4 slice. The times are simulated.
32 devices in a mesh: frames: 4 (over y, x), pix: 8 (over z, core).
Axes of the slice: x: 2, y: 2, z: 4, core: 2. Of those that a mesh axis runs over, the one named last changes fastest.
Arguments:
- photon_counts: int32 [4096, 16384], P('frames', 'pix'), may hold values from 1 to 53, as said below
- flat_field: float32 [16384], P('pix'), may hold values from 0.5 to 2
- owner_counts: int32 [8], replicated, may hold values from 512 to 2048, as said below
Outputs:
- diagonal_tiles: float32 [4096, 1024], P(('frames', 'pix'))
- offdiag_tiles: float32 [4096, 1024], P(('frames', 'pix'))
Inputs may be any that keep to these rules, and one draw needn't show every extreme that they name: owner_counts[i] is how many of owner i's 2048 slots, the first ones, hold cycle pixels; some owner holds all 2048. `photon_counts`: whole photon counts of each slot in each frame.
All inputs are finite; a program needn't handle non-finite values.
Results may differ from a plain program's by a relative error of at most 0.0003.
Values may be sent and summed in bfloat16 or wider, within the bound.
A program may use at most 64 MiB of HBM per device.

v0:
```python
import jax
import jax.numpy as jnp
from jax import lax
from jax.sharding import PartitionSpec as P


def shifted(value, axis, steps):
    count = lax.axis_size(axis)
    leading, last = (max(0, -steps), min(count, count - steps))
    return lax.ppermute(value, axis, [(source, source + steps) for source in range(leading, last)])


def gram(left, right):
    return lax.dot_general(
        left, right, (((1,), (1,)), ((), ())), preferred_element_type=jnp.float32
    )


def on_device(photon_counts, flat_field, owner_counts):
    owner_index = lax.axis_index("pix")
    slot_count = flat_field.shape[0]
    limit = owner_counts[owner_index]
    valid = (jnp.arange(slot_count, dtype=jnp.int32) < limit).astype(jnp.float32)
    weights = flat_field * valid
    pixel_total = jnp.sum(owner_counts).astype(jnp.float32)
    corrected = photon_counts.astype(jnp.float32) * weights[None, :]
    frame_sums = lax.psum(jnp.sum(corrected, axis=1), "pix")
    frame_mean = frame_sums / pixel_total
    scaled = (corrected / frame_mean[:, None]).astype(jnp.bfloat16)
    earlier = shifted(scaled, "frames", 1)
    diagonal_part = gram(scaled, scaled)
    offdiag_part = gram(scaled, earlier)
    diagonal_rows, offdiag_rows = (
        lax.psum_scatter(diagonal_part, "pix", scatter_dimension=0, tiled=True),
        lax.psum_scatter(offdiag_part, "pix", scatter_dimension=0, tiled=True),
    )
    return (diagonal_rows / pixel_total, offdiag_rows / pixel_total)


def solution(mesh):
    placed = (P("frames", "pix"), P("pix"), P())
    return jax.shard_map(
        on_device,
        mesh=mesh,
        in_specs=placed,
        out_specs=(P(("frames", "pix"), None), P(("frames", "pix"), None)),
        check_vma=False,
    )
```

profile of v0, /device:TPU:0, one launch (start us, length us, event | category | flops | bytes accessed | tf_op | source)
XLA Modules:
  0.0 204.5 jit_solution(13953203623894484739)
XLA Ops:
  7.2 0.0 reduce-scatter.3.cloned.1.call-start
  7.2 1.3 reduce_sum.19
  8.5 1.2 dynamic_slice.3
  9.7 1.3 fusion.1
  11.1 4.3 %fusion = f32[1024]{0:T(1024)S(1)} fusion(s32[1024,2048]{1,0:T(8,128)} %param.3, f32[2048]{0:T(1024)S(1)} %fusion.1), kind=kLoop, calls=%fused_computation.2 | loop fusion | flops 6290432 | bytes 8400896 | tf_op jit(solution)/shard_map/reduce_sum | solution.py:27
  15.4 18.1 %psum.7 = f32[1024]{0:T(1024)S(1)} all-reduce(f32[1024]{0:T(1024)S(1)} %fusion), channel_id=1, replica_groups=mesh['frames'=4,'pix'=8] {'pix'}, use_global_device_ids=true, to_apply=%region_1.0 | all-reduce | flops 1024 | bytes 8192 | tf_op jit(solution)/shard_map/psum | solution.py:27
  34.1 4.3 %divide_convert_fusion = bf16[1024,2048]{1,0:T(8,128)(2,1)S(1)} fusion(s32[1024,2048]{1,0:T(8,128)} %param.3, f32[1024]{0:T(1024)S(1)} %broadcast_divide_fusion.2, f32[2048]{0:T(1024)S(1)} %fusion.1), kind=kLoop, calls=%fused_computation | loop fusion | flops 8388608 | bytes 12595200 | tf_op jit(solution)/shard_map/convert_element_type | solution.py:29
  38.4 0.0 copy-start
  38.5 2.0 copy-done
  40.4 6.1 %fusion.2 = f32[1024,1024]{1,0:T(8,128)} fusion(bf16[1024,2048]{1,0:T(8,128)(2,1)S(1)} %divide_convert_fusion), kind=kOutput, calls=%fused_computation.8 | convolution fusion | flops 4294967296 | bytes 8388608 | tf_op jit(solution)/shard_map/dot_general | solution.py:14
  46.5 0.0 reduce-scatter.3.cloned.1.call-update
  46.5 0.0 reduce-scatter.5.cloned.1.call-start
  46.6 3.7 %collective-permute-start = (bf16[1024,2048]{1,0:T(8,128)(2,1)}, bf16[1024,2048]{1,0:T(8,128)(2,1)S(1)}, u32[]{:S(2)}, u32[]{:S(2)}) collective-permute-start(bf16[1024,2048]{1,0:T(8,128)(2,1)} %copy-done), channel_id=1, source_target_pairs={{0,8},{8,16},{16,24},{1,9},{9,17},{17,25},{2,10},{10,18},{18,26},{... | collective-permute-start | bytes 12582920 | tf_op jit(solution)/shard_map/ppermute | solution.py:10
  50.2 87.0 %collective-permute-done = bf16[1024,2048]{1,0:T(8,128)(2,1)S(1)} collective-permute-done((bf16[1024,2048]{1,0:T(8,128)(2,1)}, bf16[1024,2048]{1,0:T(8,128)(2,1)S(1)}, u32[]{:S(2)}, u32[]{:S(2)}) %collective-permute-start) | collective-permute-done | bytes 4194336 | tf_op jit(solution)/shard_map/ppermute | solution.py:10
  137.3 8.4 %fusion.3 = f32[1024,1024]{1,0:T(8,128)} fusion(bf16[1024,2048]{1,0:T(8,128)(2,1)} %copy-done, bf16[1024,2048]{1,0:T(8,128)(2,1)S(1)} %collective-permute-done), kind=kOutput, calls=%fused_computation.9 | convolution fusion | flops 4294967296 | bytes 12582912 | tf_op jit(solution)/shard_map/dot_general | solution.py:14
  145.6 0.0 reduce-scatter.5.cloned.1.call-update
  145.7 0.0 reduce-scatter.3.cloned.1.call-done
  145.7 1.9 broadcast_divide_fusion.1
  147.6 48.2 %reduce-scatter.5.cloned.1.call-done = f32[128,1024]{1,0:T(8,128)} async-done(((f32[1024,1024]{1,0:T(8,128)}), f32[128,1024]{1,0:T(8,128)}) %reduce-scatter.5.cloned.1.call-update) | async-done | bytes 524304 | tf_op jit(solution)/shard_map/reduce_scatter | solution.py:35
  195.8 1.9 broadcast_divide_fusion
  (1 shorter events, 0.0 us)
Async XLA Ops:
  7.2 138.5 %reduce-scatter.3.cloned.1.call-start = ((), (), s32[]{:S(2)}) async-start(), calls=%async_computation.2 | async-start | bytes 4718592 | tf_op jit(solution)/shard_map/reduce_scatter | solution.py:34
  38.4 2.0 copy-start
  46.5 149.2 %reduce-scatter.5.cloned.1.call-start = ((), (), s32[]{:S(2)}) async-start(), calls=%async_computation.3 | async-start | bytes 4718592 | tf_op jit(solution)/shard_map/reduce_scatter | solution.py:35
  46.6 90.7 %collective-permute-start = (bf16[1024,2048]{1,0:T(8,128)(2,1)}, bf16[1024,2048]{1,0:T(8,128)(2,1)S(1)}, u32[]{:S(2)}, u32[]{:S(2)}) collective-permute-start(bf16[1024,2048]{1,0:T(8,128)(2,1)} %copy-done), channel_id=1, source_target_pairs={{0,8},{8,16},{16,24},{1,9},{9,17},{17,25},{2,10},{10,18},{18,26},{... | collective-permute-start | bytes 12582920 | tf_op jit(solution)/shard_map/ppermute | solution.py:10
Sparse Core Ops, SparseCore 0:
  46.7 48.2 reduce-scatter.2
  145.8 49.9 reduce-scatter.4
where the time goes:
time: 205 us; the launch traced here: 204 us
  waiting for transfers between devices  135 us (66%)
  blocking collectives  18.1 us (9%)
  other arithmetic  15 us (7%)
  between operations  14.7 us (7%)
  matrix products  14.5 us (7%)
  starting transfers between devices  3.74 us (2%)
  local copies, waits for them, and re-layouts  3.2 us (2%)
    ppermute x1, waiting for transfers between devices, shifted(): lax.ppermute(value, axis, [(source, source + steps) for source in range(l...  87 us
    reduce_scatter x1, waiting for transfers between devices, on_device(): lax.psum_scatter(offdiag_part, 'pix', scatter_dimension=0, tiled=True)  48.2 us
    psum x1, blocking collectives, on_device(): frame_sums = lax.psum(jnp.sum(corrected, axis=1), 'pix')  18.1 us
    dot_general x2, matrix products, gram(): lax.dot_general(left, right, (((1,), (1,)), ((), ())), preferred_element_...  14.5 us
    convert_element_type x1, other arithmetic, on_device(): scaled = (corrected / frame_mean[:, None]).astype(jnp.bfloat16)  4.33 us
    reduce_sum x1, other arithmetic, on_device(): frame_sums = lax.psum(jnp.sum(corrected, axis=1), 'pix')  4.27 us
  transfers between devices with their start and end apart: 3, of which 2 were waited for; matrix products, arithmetic and copies ran while one was open for 5% of the time, Pallas kernels for 0%

commit v1 on v0

v1 whole, which is shorter than its diff:
```python
import functools

import jax
import jax.numpy as jnp
from jax import lax
from jax.experimental import pallas as pl
from jax.experimental.pallas import tpu as pltpu
from jax.sharding import PartitionSpec as P

MESH = pl.DeviceIdType.MESH
F32, BF16 = jnp.float32, jnp.bfloat16
LANES = 128
CHUNKS = 4
LEVELS = 64000.0
OFFSET = 32768
CORES = 2


def dot_rows(left, right):
    return lax.dot_general(left, right, (((1,), (1,)), ((), ())), preferred_element_type=F32)


def quantized(value):
    return ((value + 0.5).astype(jnp.int32) - OFFSET).astype(jnp.int16)


def restored(value):
    return (value.astype(jnp.int32) + OFFSET).astype(F32)


def remote(src, dst, send_sem, recv_sem, device):
    return pltpu.make_async_remote_copy(
        src_ref=src, dst_ref=dst, send_sem=send_sem, recv_sem=recv_sem,
        device_id=device, device_id_type=MESH,
    )


def kernel(
    n_frames, n_pix,
    owner_ref, counts_hbm, flat_ref, diag_ref, off_ref,
    counts, own, frames_s, weights, stats, totals, rows, cols,
    core_out, core_in, acc, z_out, z_in, last_out, last_in,
    load_sem, data_send, data_recv, stat_send, stat_recv, tot_send, tot_recv,
    core_send, core_recv, z_send, z_recv, last_send, last_recv,
):
    square = n_frames == 4
    n_z = n_pix // CORES
    stages = n_z.bit_length() - 1
    block = lax.axis_index("frames")
    pix = lax.axis_index("pix")
    z, core = pix // CORES, lax.rem(pix, CORES)
    n_rows, n_slots = counts.shape
    half = n_slots // 2
    piece = n_rows // n_pix
    step = n_rows // CHUNKS
    x = lax.rem(block, 2)
    outer = jnp.logical_or(block == 0, block == 3)
    inner = jnp.logical_not(outer)
    across = block + 1 - 2 * x
    up = lax.rem(block + 2, 4)
    me = block if square else 0
    has_next, has_prev = block < n_frames - 1, block > 0
    follow = jnp.minimum(block + 1, n_frames - 1)
    before = jnp.maximum(block - 1, 0)

    def load(q):
        part = pl.ds(q * step, step)
        return pltpu.make_async_copy(counts_hbm.at[part], counts.at[part], load_sem.at[q])

    for q in range(CHUNKS):
        load(q).start()

    barrier = pltpu.get_barrier_semaphore()
    for d in range(1, n_pix):
        pl.semaphore_signal(barrier, inc=1, device_id={"pix": lax.rem(pix + d, n_pix)}, device_id_type=MESH)
    if square:
        for d in range(1, 4):
            pl.semaphore_signal(barrier, inc=1, device_id={"frames": lax.rem(block + d, 4)}, device_id_type=MESH)
        pl.semaphore_wait(barrier, n_pix - 1 + 3)
    else:
        @pl.when(has_next)
        def _():
            pl.semaphore_signal(barrier, inc=1, device_id={"frames": follow}, device_id_type=MESH)

        @pl.when(has_prev)
        def _():
            pl.semaphore_signal(barrier, inc=1, device_id={"frames": before}, device_id_type=MESH)

        pl.semaphore_wait(barrier, n_pix - 1 + has_next.astype(jnp.int32) + has_prev.astype(jnp.int32))

    if square:
        always = block >= 0
        streams = ((0, 1 - x, across, always, always), (1, x, up, inner, outer))
    else:
        streams = ((0, 0, follow, has_next, has_prev), (1, 1, follow, has_next, has_prev))

    def data(slot, which, target, q):
        part = pl.ds(q * step, step)
        return remote(
            own.at[which, part], frames_s.at[2 + slot, part],
            data_send.at[slot, q], data_recv.at[slot, q], {"frames": target},
        )

    pixel_total = owner_ref[0]
    for i in range(1, n_pix):
        pixel_total = pixel_total + owner_ref[i]
    pixel_total = pixel_total.astype(F32)
    limit = owner_ref[pix]
    slot_ids = lax.broadcasted_iota(jnp.int32, (8, n_slots), 1)
    valid = (slot_ids < limit).astype(F32)
    weight = flat_ref[...] * valid
    weights[...] = weight
    first = weight.astype(BF16)
    rest = weight - first.astype(F32)
    second = rest.astype(BF16)
    third = (rest - second.astype(F32)).astype(BF16)
    split = (first, second, third)
    squares = (weight * weight).astype(BF16)

    stats[pix] = jnp.zeros((8, n_rows), F32)
    small = 16
    for q in range(CHUNKS):
        load(q).wait()

        @pl.loop(0, step // small)
        def _(i):
            at = pl.ds(q * step + i * small, small)
            for h in range(2):
                own[h, at, :] = counts[at, h * half:(h + 1) * half].astype(F32).astype(BF16)

        for slot, which, target, sends, _ in streams:
            @pl.when(sends)
            def _(slot=slot, which=which, target=target):
                data(slot, which, target, q).start()

    for q in range(CHUNKS):
        part = slice(q * step, (q + 1) * step)
        sums = jnp.zeros((8, step), F32)
        norms = jnp.zeros((8, step), F32)
        for h in range(2):
            held = own[h, part, :]
            lanes = slice(h * half, (h + 1) * half)
            for term in split:
                sums = sums + dot_rows(term[:, lanes], held)
            norms = norms + dot_rows(squares[:, lanes], held * held)
        stats[pix, 0:1, part] = sums[0:1]
        stats[pix, 1:2, part] = norms[0:1]

    def stat(d):
        return remote(
            stats.at[pix], stats.at[pix], stat_send.at[d], stat_recv.at[pix],
            {"pix": lax.rem(pix + d, n_pix)},
        )

    def stat_from(d):
        source = lax.rem(pix + d, n_pix)
        return remote(stats.at[source], stats.at[source], stat_send.at[d], stat_recv.at[source], {"pix": source})

    for d in range(1, n_pix):
        stat(d).start()
    for d in range(1, n_pix):
        stat_from(d).wait_recv()
    total = stats[0]
    for i in range(1, n_pix):
        total = total + stats[i]
    totals[me] = total

    if square:
        def tot(d):
            return remote(totals.at[me], totals.at[me], tot_send.at[d], tot_recv.at[me], {"frames": lax.rem(block + d, 4)})

        def tot_from(d):
            source = lax.rem(block + d, 4)
            return remote(totals.at[source], totals.at[source], tot_send.at[d], tot_recv.at[source], {"frames": source})

        for d in range(1, 4):
            tot(d).start()
    else:
        def tot_next():
            return remote(totals.at[0], totals.at[1], tot_send.at[0], tot_recv.at[0], {"frames": follow})

        @pl.when(has_next)
        def _():
            tot_next().start()

    def take(index):
        held = totals[index]
        inverse_mean = pixel_total / held[0:1]
        norm = jnp.sqrt(held[1:2]) * inverse_mean
        scale = LEVELS ** 0.5 / norm
        rows[index, 0:1, :] = scale
        rows[index, 1:2, :] = 1.0 / scale
        cols[index, 0] = jnp.transpose(jnp.broadcast_to(inverse_mean, (LANES, n_rows)))
        cols[index, 1] = jnp.transpose(jnp.broadcast_to(scale, (LANES, n_rows)))
        cols[index, 2] = jnp.transpose(jnp.broadcast_to(1.0 / scale, (LANES, n_rows)))

    take(me)

    @pl.loop(0, n_rows // small)
    def _(i):
        at = pl.ds(i * small, small)
        inverse = cols[me, 0, at, 0:1]
        for h in range(2):
            lanes = slice(h * half, (h + 1) * half)
            frame = own[h, at, :].astype(F32) * weights[0:1, lanes]
            frames_s[h, at, :] = (frame * inverse).astype(BF16)

    def product(k, pairs, row_block, col_block):
        other = 1 - core

        def core_copy(j):
            return remote(core_out.at[k, j], core_in.at[k, j], core_send.at[k, j], core_recv.at[k, j], {"pix": z * CORES + other})

        def tile(owner):
            at = pl.ds(pl.multiple_of(owner * piece, piece), piece)
            out = None
            for left, right in pairs:
                term = dot_rows(frames_s[left, at, :], frames_s[right])
                out = term if out is None else out + term
            return out

        @pl.loop(0, n_z)
        def _(j):
            core_out[k, j] = tile(j * CORES + other)
            core_copy(j).start()

        @pl.loop(0, n_z)
        def _(j):
            acc[k, j] = tile(j * CORES + core)

        @pl.loop(0, n_z)
        def _(j):
            core_copy(j).wait()
            at = pl.ds(pl.multiple_of((j * CORES + core) * piece, piece), piece)
            value = acc[k, j] + core_in[k, j]
            acc[k, j] = value * cols[row_block, 1, at, 0:1] * rows[col_block, 0:1, :]

    def z_base(s):
        return n_z - (n_z >> s)

    def z_copy(k, s, m):
        bit = 1 << s
        sign = 1 - 2 * lax.rem(z // bit, 2)
        at = z_base(s) + m
        return remote(
            z_out.at[k, at], z_in.at[k, at], z_send.at[k, at], z_recv.at[k, at],
            {"pix": (z + sign * bit) * CORES + core},
        )

    def z_send_stage(k, s):
        bit = 1 << s
        low, top = lax.rem(z, bit), lax.rem(z // bit, 2)
        for m in range(n_z >> (s + 1)):
            j = m * 2 * bit + (1 - top) * bit + low
            z_out[k, z_base(s) + m] = quantized(acc[k, j])
            z_copy(k, s, m).start()

    def z_recv_stage(k, s):
        bit = 1 << s
        for m in range(n_z >> (s + 1)):
            z_copy(k, s, m).wait()
            j = m * 2 * bit + lax.rem(z, 2 * bit)
            acc[k, j] = acc[k, j] + restored(z_in[k, z_base(s) + m])

    product(0, ((0, 0), (1, 1)), me, me)
    for s in range(stages):
        z_send_stage(0, s)
        z_recv_stage(0, s)
    mine = pl.ds(pl.multiple_of(pix * piece, piece), piece)
    inverse_total = 1.0 / jnp.full((1, 1), pixel_total, F32)
    diag_ref[...] = acc[0, z] * cols[me, 2, mine, 0:1] * (rows[me, 1:2, :] * inverse_total)

    if square:
        for d in range(1, 4):
            tot_from(d).wait_recv()
        for d in range(1, 4):
            take(lax.rem(block + d, 4))
    else:
        @pl.when(has_prev)
        def _():
            tot_next().wait_recv()
            take(1)

    for q in range(CHUNKS):
        for slot, which, target, _, arrives in streams:
            @pl.when(arrives)
            def _(slot=slot, which=which, target=target):
                data(slot, which, target, q).wait_recv()
                source = (across if slot == 0 else up) if square else 1
                lanes = pl.ds(pl.multiple_of((x if square else slot) * half, half), half)

                @pl.loop(0, step // small)
                def _(i):
                    at = pl.ds(q * step + i * small, small)
                    inverse = cols[source, 0, at, 0:1]
                    frame = frames_s[2 + slot, at, :].astype(F32) * weights[0:1, lanes]
                    frames_s[2 + slot, at, :] = (frame * inverse).astype(BF16)

    if square:
        later, sooner = jnp.maximum(block, across), jnp.minimum(block, across)
        product(1, ((jnp.where(x == 0, 2, 1), jnp.where(x == 0, 0, 2)),), later, sooner)

        @pl.when(outer)
        def _():
            product(2, ((jnp.where(x == 0, 3, 2), jnp.where(x == 0, 2, 3)),), 2, 1)

        for s in range(stages):
            z_send_stage(1, s)

            @pl.when(outer)
            def _():
                z_send_stage(2, s)

            z_recv_stage(1, s)

            @pl.when(outer)
            def _():
                z_recv_stage(2, s)

        even = x == 0

        def last(source, slot, target):
            return remote(last_out.at[source], last_in.at[slot], last_send.at[source], last_recv.at[slot], {"frames": target})

        @pl.when(even)
        def _():
            last_out[0] = quantized(acc[1, z])
            last(0, 0, across).start()

        @pl.when(block == 0)
        def _():
            last_out[1] = quantized(acc[2, z])
            last(1, 1, up).start()

        @pl.when(block == 3)
        def _():
            last_out[1] = quantized(acc[2, z])
            last(1, 0, across).start()

        @pl.when(block == 0)
        def _():
            off_ref[...] = jnp.zeros_like(off_ref)

        def write(value):
            off_ref[...] = value * cols[block, 2, mine, 0:1] * (rows[before, 1:2, :] * inverse_total)

        @pl.when(x == 1)
        def _():
            last(0, 0, across).wait_recv()
            write(acc[1, z] + restored(last_in[0]))

        @pl.when(block == 2)
        def _():
            last(0, 0, across).wait_recv()
            last(1, 1, up).wait_recv()
            write(restored(last_in[0]) + restored(last_in[1]))

        @pl.when(even)
        def _():
            last(0, 0, across).wait_send()

        @pl.when(outer)
        def _():
            last(1, 1, up).wait_send()
    else:
        @pl.when(has_prev)
        def _():
            product(1, ((0, 2), (1, 3)), 0, 1)
            for s in range(stages):
                z_send_stage(1, s)
                z_recv_stage(1, s)
            off_ref[...] = acc[1, z] * cols[0, 2, mine, 0:1] * (rows[1, 1:2, :] * inverse_total)

        @pl.when(jnp.logical_not(has_prev))
        def _():
            off_ref[...] = jnp.zeros_like(off_ref)

    for d in range(1, n_pix):
        stat(d).wait_send()
    if square:
        for d in range(1, 4):
            tot(d).wait_send()
    else:
        @pl.when(has_next)
        def _():
            tot_next().wait_send()
    for q in range(CHUNKS):
        for slot, which, target, sends, _ in streams:
            @pl.when(sends)
            def _(slot=slot, which=which, target=target):
                data(slot, which, target, q).wait_send()


def on_device(n_frames, n_pix, photon_counts, flat_field, owner_counts):
    n_rows, n_slots = photon_counts.shape
    half, piece, n_z = n_slots // 2, n_rows // n_pix, n_pix // CORES
    tiles, blocks = (3, 4) if n_frames == 4 else (2, 2)
    sent = max(n_z - 1, 1)
    flat = jnp.broadcast_to(flat_field[None, :], (8, n_slots))
    out = jax.ShapeDtypeStruct((piece, n_rows), F32)
    dma = pltpu.SemaphoreType.DMA
    return pl.pallas_call(
        functools.partial(kernel, n_frames, n_pix),
        out_shape=(out, out),
        in_specs=[
            pl.BlockSpec(memory_space=pltpu.SMEM),
            pl.BlockSpec(memory_space=pl.ANY),
            pl.BlockSpec(memory_space=pltpu.VMEM),
        ],
        out_specs=(pl.BlockSpec(memory_space=pltpu.VMEM),) * 2,
        scratch_shapes=[
            pltpu.VMEM((n_rows, n_slots), jnp.int32),
            pltpu.VMEM((2, n_rows, half), BF16),
            pltpu.VMEM((4, n_rows, half), BF16),
            pltpu.VMEM((8, n_slots), F32),
            pltpu.VMEM((n_pix, 8, n_rows), F32),
            pltpu.VMEM((blocks, 8, n_rows), F32),
            pltpu.VMEM((blocks, 8, n_rows), F32),
            pltpu.VMEM((blocks, 3, n_rows, LANES), F32),
            pltpu.VMEM((tiles, n_z, piece, n_rows), F32),
            pltpu.VMEM((tiles, n_z, piece, n_rows), F32),
            pltpu.VMEM((tiles, n_z, piece, n_rows), F32),
            pltpu.VMEM((tiles, sent, piece, n_rows), jnp.int16),
            pltpu.VMEM((tiles, sent, piece, n_rows), jnp.int16),
            pltpu.VMEM((2, piece, n_rows), jnp.int16),
            pltpu.VMEM((2, piece, n_rows), jnp.int16),
            dma((CHUNKS,)),
            dma((2, CHUNKS)), dma((2, CHUNKS)),
            dma((n_pix,)), dma((n_pix,)),
            dma((4,)), dma((4,)),
            dma((tiles, n_z)), dma((tiles, n_z)),
            dma((tiles, sent)), dma((tiles, sent)),
            dma((2,)), dma((2,)),
        ],
        compiler_params=pltpu.CompilerParams(
            collective_id=0, has_side_effects=True, vmem_limit_bytes=62 * 1024 * 1024
        ),
        cost_estimate=pl.CostEstimate(
            flops=4 * n_rows * n_rows * n_slots, bytes_accessed=4 * n_rows * n_slots, transcendentals=0
        ),
    )(owner_counts, photon_counts, flat)


def solution(mesh):
    return jax.shard_map(
        functools.partial(on_device, mesh.shape["frames"], mesh.shape["pix"]),
        mesh=mesh,
        in_specs=(P("frames", "pix"), P("pix"), P()),
        out_specs=(P(("frames", "pix"), None), P(("frames", "pix"), None)),
        check_vma=False,
    )
```

time: 205 us -> 151 us (0.74)
  Pallas kernels: 0 us -> 144 us
  waiting for transfers between devices: 135 us -> 0 us
  blocking collectives: 18.1 us -> 0 us
  other arithmetic: 15 us -> 0 us
  matrix products: 14.5 us -> 0 us
  between operations: 14.7 us -> 0.64 us
  starting transfers between devices: 3.74 us -> 0 us
    pallas_call x0 -> x1, Pallas kernels: none -> 144 us  [on_device(): pl.pallas_call(functools.partial(kernel, n_frames, n_pix), out_shape=(out...]
    ppermute x1 -> x0, waiting for transfers between devices: 87 us -> none  [shifted(): lax.ppermute(value, axis, [(source, source + steps) for source in range(l...]
    reduce_scatter x2 -> x0, waiting for transfers between devices: 48.2 us -> none  [the longest x1 48.2 us: on_device(): lax.psum_scatter(offdiag_part, 'pix', scatter_dimension=0, tiled=True)]
    psum x1 -> x0, blocking collectives: 18.1 us -> none  [on_device(): frame_sums = lax.psum(jnp.sum(corrected, axis=1), 'pix')]
    dot_general x2 -> x0, matrix products: 14.5 us -> none  [gram(): lax.dot_general(left, right, (((1,), (1,)), ((), ())), preferred_element_...]
    reduce_sum x2 -> x0, other arithmetic: 5.56 us -> none  [the longest x1 4.27 us: on_device(): frame_sums = lax.psum(jnp.sum(corrected, axis=1), 'pix')]
    convert_element_type x1 -> x0, other arithmetic: 4.33 us -> none  [on_device(): scaled = (corrected / frame_mean[:, None]).astype(jnp.bfloat16)]
    div x3 -> x0, other arithmetic: 3.79 us -> none  [the longest x2 3.79 us: on_device(): return (diagonal_rows / pixel_total, offdiag_rows / pixel_total)]
  transfers between devices with their start and end apart: 3 -> 0, of which waited for: 2 -> 0; matrix products, arithmetic and copies ran while one was open for 5% -> 0% of each run, Pallas kernels for 0% -> 0%
where the time goes in v1:
time: 151 us; the launch traced here: 150 us
  Pallas kernels  144 us (95%)
  local copies, waits for them, and re-layouts  5.1 us (3%)
    pallas_call x1, Pallas kernels, on_device(): pl.pallas_call(functools.partial(kernel, n_frames, n_pix), out_shape=(out...  144 us
    unnamed x2, local copies, waits for them, and re-layouts  3.77 us

profile of v1, /device:TPU:0, one launch (start us, length us, event | category | flops | bytes accessed | tf_op | source)
XLA Modules:
  0.0 149.9 jit_solution(76086617009809069)
XLA Ops:
  0.6 1.3 broadcast_in_dim.2.flat_ref
  2.0 144.1 %shard_map.50 = (f32[128,1024]{1,0:T(8,128)}, f32[128,1024]{1,0:T(8,128)}) custom-call(s32[8]{0:T(128)} %owner_ref.1, s32[1024,2048]{1,0:T(8,128)} %counts_hbm.1, f32[8,2048]{1,0:T(8,128)} %broadcast_in_dim.2.flat_ref), custom_call_target="tpu_custom_call" | custom-call | flops 8589934592 | bytes 8388608 | tf_op jit(solution)/shard_map/pallas_call | solution.py:402
  146.1 1.9 %copy.7 = f32[128,1024]{1,0:T(8,128)} copy(f32[128,1024]{1,0:T(8,128)} %get-tuple-element.4) | data formatting | bytes 1048576
  148.0 1.9 %copy.8 = f32[128,1024]{1,0:T(8,128)} copy(f32[128,1024]{1,0:T(8,128)} %get-tuple-element.5) | data formatting | bytes 1048576

commit v2 on v1

--- a/solution.py
+++ b/solution.py
@@ -10,7 +10,6 @@
 MESH = pl.DeviceIdType.MESH
 F32, BF16 = jnp.float32, jnp.bfloat16
 LANES = 128
-CHUNKS = 4
 LEVELS = 64000.0
 OFFSET = 32768
 CORES = 2
@@ -18,6 +17,11 @@
 
 def dot_rows(left, right):
     return lax.dot_general(left, right, (((1,), (1,)), ((), ())), preferred_element_type=F32)
+
+
+def widened(column, lanes):
+    count = lanes // LANES
+    return column if count == 1 else jnp.concatenate([column] * count, axis=-1)
 
 
 def quantized(value):
@@ -38,7 +42,7 @@
 def kernel(
     n_frames, n_pix,
     owner_ref, counts_hbm, flat_ref, diag_ref, off_ref,
-    counts, own, frames_s, weights, stats, totals, rows, cols,
+    counts, own, frames_s, sum_rows, weights, stats, totals, rows, cols,
     core_out, core_in, acc, z_out, z_in, last_out, last_in,
     load_sem, data_send, data_recv, stat_send, stat_recv, tot_send, tot_recv,
     core_send, core_recv, z_send, z_recv, last_send, last_recv,
@@ -52,7 +56,7 @@
     n_rows, n_slots = counts.shape
     half = n_slots // 2
     piece = n_rows // n_pix
-    step = n_rows // CHUNKS
+    pair = CORES * piece
     x = lax.rem(block, 2)
     outer = jnp.logical_or(block == 0, block == 3)
     inner = jnp.logical_not(outer)
@@ -64,10 +68,10 @@
     before = jnp.maximum(block - 1, 0)
 
     def load(q):
-        part = pl.ds(q * step, step)
+        part = pl.ds(q * pair, pair)
         return pltpu.make_async_copy(counts_hbm.at[part], counts.at[part], load_sem.at[q])
 
-    for q in range(CHUNKS):
+    for q in range(n_z):
         load(q).start()
 
     barrier = pltpu.get_barrier_semaphore()
@@ -95,9 +99,8 @@
         streams = ((0, 0, follow, has_next, has_prev), (1, 1, follow, has_next, has_prev))
 
     def data(slot, which, target, q):
-        part = pl.ds(q * step, step)
         return remote(
-            own.at[which, part], frames_s.at[2 + slot, part],
+            own.at[which, q], frames_s.at[2 + slot, q],
             data_send.at[slot, q], data_recv.at[slot, q], {"frames": target},
         )
 
@@ -106,45 +109,48 @@
         pixel_total = pixel_total + owner_ref[i]
     pixel_total = pixel_total.astype(F32)
     limit = owner_ref[pix]
-    slot_ids = lax.broadcasted_iota(jnp.int32, (8, n_slots), 1)
+    slot_ids = lax.broadcasted_iota(jnp.int32, (16, n_slots), 1)
     valid = (slot_ids < limit).astype(F32)
     weight = flat_ref[...] * valid
     weights[...] = weight
-    first = weight.astype(BF16)
-    rest = weight - first.astype(F32)
-    second = rest.astype(BF16)
-    third = (rest - second.astype(F32)).astype(BF16)
-    split = (first, second, third)
-    squares = (weight * weight).astype(BF16)
+    first = weight.astype(BF16).astype(F32)
+    second = (weight - first).astype(BF16).astype(F32)
+    third = weight - first - second
+    line = lax.broadcasted_iota(jnp.int32, (16, n_slots), 0)
+    none = jnp.zeros_like(weight)
+    split = jnp.where(line == 0, first, jnp.where(line == 1, second, jnp.where(line == 2, third, none)))
+    filler = jnp.zeros((LANES - 16, n_slots), BF16)
+    for i, value in enumerate((split, jnp.where(line == 3, weight * weight, none))):
+        sum_rows[i, 0:16, :] = value.astype(BF16)
+        sum_rows[i, 16:LANES, :] = filler
 
     stats[pix] = jnp.zeros((8, n_rows), F32)
     small = 16
-    for q in range(CHUNKS):
+    for q in range(n_z):
         load(q).wait()
 
-        @pl.loop(0, step // small)
+        @pl.loop(0, piece // small)
         def _(i):
-            at = pl.ds(q * step + i * small, small)
-            for h in range(2):
-                own[h, at, :] = counts[at, h * half:(h + 1) * half].astype(F32).astype(BF16)
+            for c in range(CORES):
+                for h in range(2):
+                    taken = counts[pl.ds(q * pair + c * piece + i * small, small), h * half:(h + 1) * half]
+                    own[h, q, c, pl.ds(i * small, small), :] = taken.astype(F32).astype(BF16)
 
         for slot, which, target, sends, _ in streams:
             @pl.when(sends)
             def _(slot=slot, which=which, target=target):
                 data(slot, which, target, q).start()
 
-    for q in range(CHUNKS):
-        part = slice(q * step, (q + 1) * step)
-        sums = jnp.zeros((8, step), F32)
-        norms = jnp.zeros((8, step), F32)
+    for q in range(n_z):
+        sums = jnp.zeros((pair, LANES), F32)
         for h in range(2):
-            held = own[h, part, :]
+            held = own[h, q].reshape(pair, half)
             lanes = slice(h * half, (h + 1) * half)
-            for term in split:
-                sums = sums + dot_rows(term[:, lanes], held)
-            norms = norms + dot_rows(squares[:, lanes], held * held)
-        stats[pix, 0:1, part] = sums[0:1]
-        stats[pix, 1:2, part] = norms[0:1]
+            sums = sums + dot_rows(held, sum_rows[0, :, lanes]) + dot_rows(held * held, sum_rows[1, :, lanes])
+        sums = jnp.transpose(sums)
+        part = slice(q * pair, (q + 1) * pair)
+        stats[pix, 0:1, part] = sums[0:1] + sums[1:2] + sums[2:3]
+        stats[pix, 1:2, part] = sums[3:4]
 
     def stat(d):
         return remote(
@@ -190,50 +196,62 @@
         scale = LEVELS ** 0.5 / norm
         rows[index, 0:1, :] = scale
         rows[index, 1:2, :] = 1.0 / scale
-        cols[index, 0] = jnp.transpose(jnp.broadcast_to(inverse_mean, (LANES, n_rows)))
-        cols[index, 1] = jnp.transpose(jnp.broadcast_to(scale, (LANES, n_rows)))
-        cols[index, 2] = jnp.transpose(jnp.broadcast_to(1.0 / scale, (LANES, n_rows)))
+        for i, value in enumerate((inverse_mean, scale, 1.0 / scale)):
+            column = jnp.transpose(jnp.broadcast_to(value, (LANES, n_rows)))
+            cols[index, i] = column.reshape(n_z, CORES, piece, LANES)
 
     take(me)
 
-    @pl.loop(0, n_rows // small)
-    def _(i):
-        at = pl.ds(i * small, small)
-        inverse = cols[me, 0, at, 0:1]
-        for h in range(2):
-            lanes = slice(h * half, (h + 1) * half)
-            frame = own[h, at, :].astype(F32) * weights[0:1, lanes]
-            frames_s[h, at, :] = (frame * inverse).astype(BF16)
+    def scale_frames(src, src_index, dst_index, first_lane, q, index):
+        @pl.loop(0, piece // small)
+        def _(i):
+            at = pl.ds(i * small, small)
+            for c in range(CORES):
+                inverse = cols[index, 0, q, c, at, :]
+                for g in range(0, half, LANES):
+                    weight = weights[0:1, pl.ds(pl.multiple_of(first_lane + g, LANES), LANES)]
+                    frame = src[src_index, q, c, at, g:g + LANES].astype(F32) * weight
+                    frames_s[dst_index, q, c, at, g:g + LANES] = (frame * inverse).astype(BF16)
+
+    for h in range(2):
+        @pl.loop(0, n_z)
+        def _(q):
+            scale_frames(own, h, h, h * half, q, me)
 
     def product(k, pairs, row_block, col_block):
         other = 1 - core
 
-        def core_copy(j):
-            return remote(core_out.at[k, j], core_in.at[k, j], core_send.at[k, j], core_recv.at[k, j], {"pix": z * CORES + other})
-
-        def tile(owner):
-            at = pl.ds(pl.multiple_of(owner * piece, piece), piece)
+        def at(n):
+            return pl.ds(pl.multiple_of(n * pair, LANES), pair)
+
+        def core_copy(n):
+            return remote(
+                core_out.at[k, :, :, at(n)], core_in.at[k, :, :, at(n)],
+                core_send.at[k, n], core_recv.at[k, n], {"pix": z * CORES + other},
+            )
+
+        def tile(side, n):
             out = None
             for left, right in pairs:
-                term = dot_rows(frames_s[left, at, :], frames_s[right])
+                term = dot_rows(
+                    frames_s[left, :, side].reshape(n_z * piece, half),
+                    frames_s[right, n].reshape(pair, half),
+                )
                 out = term if out is None else out + term
-            return out
+            return out.reshape(n_z, piece, pair)
 
         @pl.loop(0, n_z)
-        def _(j):
-            core_out[k, j] = tile(j * CORES + other)
-            core_copy(j).start()
+        def _(n):
+            core_out[k, :, :, at(n)] = tile(other, n)
+            core_copy(n).start()
 
         @pl.loop(0, n_z)
-        def _(j):
-            acc[k, j] = tile(j * CORES + core)
-
-        @pl.loop(0, n_z)
-        def _(j):
-            core_copy(j).wait()
-            at = pl.ds(pl.multiple_of((j * CORES + core) * piece, piece), piece)
-            value = acc[k, j] + core_in[k, j]
-            acc[k, j] = value * cols[row_block, 1, at, 0:1] * rows[col_block, 0:1, :]
+        def _(n):
+            value = tile(core, n)
+            core_copy(n).wait()
+            value = value + core_in[k, :, :, at(n)]
+            value = value * widened(cols[row_block, 1, :, core], pair)
+            acc[k, :, :, at(n)] = value * rows[col_block, 0:1, at(n)]
 
     def z_base(s):
         return n_z - (n_z >> s)
@@ -266,9 +284,8 @@
     for s in range(stages):
         z_send_stage(0, s)
         z_recv_stage(0, s)
-    mine = pl.ds(pl.multiple_of(pix * piece, piece), piece)
     inverse_total = 1.0 / jnp.full((1, 1), pixel_total, F32)
-    diag_ref[...] = acc[0, z] * cols[me, 2, mine, 0:1] * (rows[me, 1:2, :] * inverse_total)
+    diag_ref[...] = acc[0, z] * widened(cols[me, 2, z, core], n_rows) * (rows[me, 1:2, :] * inverse_total)
 
     if square:
         for d in range(1, 4):
@@ -281,20 +298,13 @@
             tot_next().wait_recv()
             take(1)
 
-    for q in range(CHUNKS):
+    for q in range(n_z):
         for slot, which, target, _, arrives in streams:
             @pl.when(arrives)
             def _(slot=slot, which=which, target=target):
                 data(slot, which, target, q).wait_recv()
                 source = (across if slot == 0 else up) if square else 1
-                lanes = pl.ds(pl.multiple_of((x if square else slot) * half, half), half)
-
-                @pl.loop(0, step // small)
-                def _(i):
-                    at = pl.ds(q * step + i * small, small)
-                    inverse = cols[source, 0, at, 0:1]
-                    frame = frames_s[2 + slot, at, :].astype(F32) * weights[0:1, lanes]
-                    frames_s[2 + slot, at, :] = (frame * inverse).astype(BF16)
+                scale_frames(frames_s, 2 + slot, 2 + slot, (x if square else slot) * half, q, source)
 
     if square:
         later, sooner = jnp.maximum(block, across), jnp.minimum(block, across)
@@ -342,7 +352,7 @@
             off_ref[...] = jnp.zeros_like(off_ref)
 
         def write(value):
-            off_ref[...] = value * cols[block, 2, mine, 0:1] * (rows[before, 1:2, :] * inverse_total)
+            off_ref[...] = value * widened(cols[block, 2, z, core], n_rows) * (rows[before, 1:2, :] * inverse_total)
 
         @pl.when(x == 1)
         def _():
@@ -369,7 +379,7 @@
             for s in range(stages):
                 z_send_stage(1, s)
                 z_recv_stage(1, s)
-            off_ref[...] = acc[1, z] * cols[0, 2, mine, 0:1] * (rows[1, 1:2, :] * inverse_total)
+            off_ref[...] = acc[1, z] * widened(cols[0, 2, z, core], n_rows) * (rows[1, 1:2, :] * inverse_total)
 
         @pl.when(jnp.logical_not(has_prev))
         def _():
@@ -384,7 +394,7 @@
         @pl.when(has_next)
         def _():
             tot_next().wait_send()
-    for q in range(CHUNKS):
+    for q in range(n_z):
         for slot, which, target, sends, _ in streams:
             @pl.when(sends)
             def _(slot=slot, which=which, target=target):
@@ -396,7 +406,7 @@
     half, piece, n_z = n_slots // 2, n_rows // n_pix, n_pix // CORES
     tiles, blocks = (3, 4) if n_frames == 4 else (2, 2)
     sent = max(n_z - 1, 1)
-    flat = jnp.broadcast_to(flat_field[None, :], (8, n_slots))
+    flat = flat_field[None, :]
     out = jax.ShapeDtypeStruct((piece, n_rows), F32)
     dma = pltpu.SemaphoreType.DMA
     return pl.pallas_call(
@@ -410,13 +420,14 @@
         out_specs=(pl.BlockSpec(memory_space=pltpu.VMEM),) * 2,
         scratch_shapes=[
             pltpu.VMEM((n_rows, n_slots), jnp.int32),
-            pltpu.VMEM((2, n_rows, half), BF16),
-            pltpu.VMEM((4, n_rows, half), BF16),
-            pltpu.VMEM((8, n_slots), F32),
+            pltpu.VMEM((2, n_z, CORES, piece, half), BF16),
+            pltpu.VMEM((4, n_z, CORES, piece, half), BF16),
+            pltpu.VMEM((2, LANES, n_slots), BF16),
+            pltpu.VMEM((16, n_slots), F32),
             pltpu.VMEM((n_pix, 8, n_rows), F32),
             pltpu.VMEM((blocks, 8, n_rows), F32),
             pltpu.VMEM((blocks, 8, n_rows), F32),
-            pltpu.VMEM((blocks, 3, n_rows, LANES), F32),
+            pltpu.VMEM((blocks, 3, n_z, CORES, piece, LANES), F32),
             pltpu.VMEM((tiles, n_z, piece, n_rows), F32),
             pltpu.VMEM((tiles, n_z, piece, n_rows), F32),
             pltpu.VMEM((tiles, n_z, piece, n_rows), F32),
@@ -424,8 +435,8 @@
             pltpu.VMEM((tiles, sent, piece, n_rows), jnp.int16),
             pltpu.VMEM((2, piece, n_rows), jnp.int16),
             pltpu.VMEM((2, piece, n_rows), jnp.int16),
-            dma((CHUNKS,)),
-            dma((2, CHUNKS)), dma((2, CHUNKS)),
+            dma((n_z,)),
+            dma((2, n_z)), dma((2, n_z)),
             dma((n_pix,)), dma((n_pix,)),
             dma((4,)), dma((4,)),
             dma((tiles, n_z)), dma((tiles, n_z)),

time: 151 us -> 128 us (0.85)
  Pallas kernels: 144 us -> 123 us
    pallas_call x1, Pallas kernels: 144 us -> 123 us  [on_device(): pl.pallas_call(functools.partial(kernel, n_frames, n_pix), out_shape=(out...]
where the time goes in v2:
time: 128 us
  Pallas kernels  123 us (96%)
  local copies, waits for them, and re-layouts  3.77 us (3%)
    pallas_call x1, Pallas kernels, on_device(): pl.pallas_call(functools.partial(kernel, n_frames, n_pix), out_shape=(out...  123 us
    unnamed x2, local copies, waits for them, and re-layouts  3.77 us

profile of v2, /device:TPU:0, one launch (start us, length us, event | category | flops | bytes accessed | tf_op | source)
XLA Modules:
  0.0 127.7 jit_solution(7613606933956509718)
XLA Ops:
  0.6 123.3 %shard_map.50 = (f32[128,1024]{1,0:T(8,128)}, f32[128,1024]{1,0:T(8,128)}) custom-call(s32[8]{0:T(128)} %owner_ref.1, s32[1024,2048]{1,0:T(8,128)} %counts_hbm.1, f32[1,2048]{1,0:T(1,128)} %bitcast.1), custom_call_target="tpu_custom_call" | custom-call | flops 8589934592 | bytes 8388608 | tf_op jit(solution)/shard_map/pallas_call | solution.py:412
  123.9 1.9 %copy.7 = f32[128,1024]{1,0:T(8,128)} copy(f32[128,1024]{1,0:T(8,128)} %get-tuple-element.4) | data formatting | bytes 1048576
  125.8 1.9 %copy.8 = f32[128,1024]{1,0:T(8,128)} copy(f32[128,1024]{1,0:T(8,128)} %get-tuple-element.5) | data formatting | bytes 1048576

commit v3 on v2

--- a/solution.py
+++ b/solution.py
@@ -280,25 +280,17 @@
             j = m * 2 * bit + lax.rem(z, 2 * bit)
             acc[k, j] = acc[k, j] + restored(z_in[k, z_base(s) + m])
 
-    product(0, ((0, 0), (1, 1)), me, me)
-    for s in range(stages):
-        z_send_stage(0, s)
-        z_recv_stage(0, s)
-    inverse_total = 1.0 / jnp.full((1, 1), pixel_total, F32)
-    diag_ref[...] = acc[0, z] * widened(cols[me, 2, z, core], n_rows) * (rows[me, 1:2, :] * inverse_total)
-
-    if square:
-        for d in range(1, 4):
-            tot_from(d).wait_recv()
-        for d in range(1, 4):
-            take(lax.rem(block + d, 4))
-    else:
-        @pl.when(has_prev)
-        def _():
-            tot_next().wait_recv()
-            take(1)
-
-    for q in range(n_z):
+    def diag_steps(first_stage, end_stage):
+        for s in range(max(first_stage, 0), end_stage):
+            z_recv_stage(0, s)
+            if s + 1 < stages:
+                z_send_stage(0, s + 1)
+
+    def finish_diag():
+        diag_steps(stages - 1, stages)
+        diag_ref[...] = acc[0, z] * widened(cols[me, 2, z, core], n_rows) * (rows[me, 1:2, :] * inverse_total)
+
+    def receive(q):
         for slot, which, target, _, arrives in streams:
             @pl.when(arrives)
             def _(slot=slot, which=which, target=target):
@@ -306,53 +298,81 @@
                 source = (across if slot == 0 else up) if square else 1
                 scale_frames(frames_s, 2 + slot, 2 + slot, (x if square else slot) * half, q, source)
 
-    if square:
+    inverse_total = 1.0 / jnp.full((1, 1), pixel_total, F32)
+    product(0, ((0, 0), (1, 1)), me, me)
+    if stages:
+        z_send_stage(0, 0)
+
+    if square:
+        for d in range(1, 4):
+            tot_from(d).wait_recv()
+        for d in range(1, 4):
+            take(lax.rem(block + d, 4))
+    else:
+        @pl.when(has_prev)
+        def _():
+            tot_next().wait_recv()
+            take(1)
+
+    for q in range(n_z - 1):
+        receive(q)
+    diag_steps(0, stages - 1)
+    receive(n_z - 1)
+
+    if square:
+        even = x == 0
         later, sooner = jnp.maximum(block, across), jnp.minimum(block, across)
-        product(1, ((jnp.where(x == 0, 2, 1), jnp.where(x == 0, 0, 2)),), later, sooner)
-
-        @pl.when(outer)
-        def _():
-            product(2, ((jnp.where(x == 0, 3, 2), jnp.where(x == 0, 2, 3)),), 2, 1)
-
-        for s in range(stages):
-            z_send_stage(1, s)
-
-            @pl.when(outer)
-            def _():
-                z_send_stage(2, s)
-
-            z_recv_stage(1, s)
-
-            @pl.when(outer)
-            def _():
-                z_recv_stage(2, s)
-
-        even = x == 0
 
         def last(source, slot, target):
             return remote(last_out.at[source], last_in.at[slot], last_send.at[source], last_recv.at[slot], {"frames": target})
 
-        @pl.when(even)
-        def _():
-            last_out[0] = quantized(acc[1, z])
-            last(0, 0, across).start()
-
-        @pl.when(block == 0)
-        def _():
-            last_out[1] = quantized(acc[2, z])
-            last(1, 1, up).start()
-
-        @pl.when(block == 3)
-        def _():
-            last_out[1] = quantized(acc[2, z])
-            last(1, 0, across).start()
-
-        @pl.when(block == 0)
-        def _():
-            off_ref[...] = jnp.zeros_like(off_ref)
+        def send_last(k):
+            if k == 1:
+                @pl.when(even)
+                def _():
+                    last_out[0] = quantized(acc[1, z])
+                    last(0, 0, across).start()
+            else:
+                last_out[1] = quantized(acc[2, z])
+
+                @pl.when(block == 0)
+                def _():
+                    last(1, 1, up).start()
+
+                @pl.when(block == 3)
+                def _():
+                    last(1, 0, across).start()
+
+        def advance(k, s):
+            if s >= 0:
+                z_recv_stage(k, s)
+            if s + 1 < stages:
+                z_send_stage(k, s + 1)
+            else:
+                send_last(k)
+
+        product(1, ((jnp.where(even, 2, 1), jnp.where(even, 0, 2)),), later, sooner)
+        advance(1, -1)
+
+        @pl.when(outer)
+        def _():
+            product(2, ((jnp.where(even, 3, 2), jnp.where(even, 2, 3)),), 2, 1)
+            advance(2, -1)
+
+        finish_diag()
+        for s in range(stages):
+            advance(1, s)
+
+            @pl.when(outer)
+            def _(s=s):
+                advance(2, s)
 
         def write(value):
             off_ref[...] = value * widened(cols[block, 2, z, core], n_rows) * (rows[before, 1:2, :] * inverse_total)
+
+        @pl.when(block == 0)
+        def _():
+            off_ref[...] = jnp.zeros_like(off_ref)
 
         @pl.when(x == 1)
         def _():
@@ -384,6 +404,8 @@
         @pl.when(jnp.logical_not(has_prev))
         def _():
             off_ref[...] = jnp.zeros_like(off_ref)
+
+        finish_diag()
 
     for d in range(1, n_pix):
         stat(d).wait_send()

time: 128 us -> 121 us (0.945)
  Pallas kernels: 123 us -> 116 us
    pallas_call x1, Pallas kernels: 123 us -> 116 us  [on_device(): pl.pallas_call(functools.partial(kernel, n_frames, n_pix), out_shape=(out...]
where the time goes in v3:
time: 121 us
  Pallas kernels  116 us (96%)
  local copies, waits for them, and re-layouts  3.77 us (3%)
    pallas_call x1, Pallas kernels, on_device(): pl.pallas_call(functools.partial(kernel, n_frames, n_pix), out_shape=(out...  116 us
    unnamed x2, local copies, waits for them, and re-layouts  3.77 us

profile of v3, /device:TPU:0, one launch (start us, length us, event | category | flops | bytes accessed | tf_op | source)
XLA Modules:
  0.0 120.9 jit_solution(8931212596850936927)
XLA Ops:
  0.6 116.4 %shard_map.50 = (f32[128,1024]{1,0:T(8,128)}, f32[128,1024]{1,0:T(8,128)}) custom-call(s32[8]{0:T(128)} %owner_ref.1, s32[1024,2048]{1,0:T(8,128)} %counts_hbm.1, f32[1,2048]{1,0:T(1,128)} %bitcast.1), custom_call_target="tpu_custom_call" | custom-call | flops 8589934592 | bytes 8388608 | tf_op jit(solution)/shard_map/pallas_call | solution.py:434
  117.1 1.9 %copy.7 = f32[128,1024]{1,0:T(8,128)} copy(f32[128,1024]{1,0:T(8,128)} %get-tuple-element.4) | data formatting | bytes 1048576
  119.0 1.9 %copy.8 = f32[128,1024]{1,0:T(8,128)} copy(f32[128,1024]{1,0:T(8,128)} %get-tuple-element.5) | data formatting | bytes 1048576

commit v4 on v2

--- a/solution.py
+++ b/solution.py
@@ -43,7 +43,7 @@
     n_frames, n_pix,
     owner_ref, counts_hbm, flat_ref, diag_ref, off_ref,
     counts, own, frames_s, sum_rows, weights, stats, totals, rows, cols,
-    core_out, core_in, acc, z_out, z_in, last_out, last_in,
+    prod, core_in, z_out, z_in, last_out, last_in,
     load_sem, data_send, data_recv, stat_send, stat_recv, tot_send, tot_recv,
     core_send, core_recv, z_send, z_recv, last_send, last_recv,
 ):
@@ -218,74 +218,126 @@
         def _(q):
             scale_frames(own, h, h, h * half, q, me)
 
+    other = 1 - core
+    everything = slice(None)
+
+    def lanes_of(n):
+        return pl.ds(n * pair, pair)
+
+    def core_columns(k, n):
+        return remote(
+            prod.at[k, :, other, :, lanes_of(n)], core_in.at[k, :, :, lanes_of(n)],
+            core_send.at[k, n], core_recv.at[k, n], {"pix": z * CORES + other},
+        )
+
+    def core_rows(k, j):
+        return remote(
+            prod.at[k, j, other], core_in.at[k, j],
+            core_send.at[k, j], core_recv.at[k, j], {"pix": z * CORES + other},
+        )
+
+    def multiply_columns(k, pairs, n):
+        out = None
+        for left, right in pairs:
+            term = dot_rows(frames_s[left].reshape(n_rows, half), frames_s[right, n].reshape(pair, half))
+            out = term if out is None else out + term
+        prod[k, :, :, :, lanes_of(n)] = out.reshape(n_z, CORES, piece, pair)
+        core_columns(k, n).start()
+
+    def merge_columns(k, n, row_block, col_block):
+        core_columns(k, n).wait()
+        value = prod[k, :, core, :, lanes_of(n)] + core_in[k, :, :, lanes_of(n)]
+        value = value * widened(cols[row_block, 1, :, core], pair)
+        prod[k, :, core, :, lanes_of(n)] = value * rows[col_block, 0:1, lanes_of(n)]
+
+    def multiply_rows(k, left, right, j):
+        for n in range(n_z):
+            out = dot_rows(frames_s[left, j].reshape(pair, half), frames_s[right, n].reshape(pair, half))
+            prod[k, j, :, :, lanes_of(n)] = out.reshape(CORES, piece, pair)
+        core_rows(k, j).start()
+
+    def merge_rows(k, j, row_block, col_block):
+        core_rows(k, j).wait()
+        value = (prod[k, j, core] + core_in[k, j]) * widened(cols[row_block, 1, j, core], n_rows)
+        prod[k, j, core] = value * rows[col_block, 0:1, :]
+
     def product(k, pairs, row_block, col_block):
-        other = 1 - core
-
-        def at(n):
-            return pl.ds(pl.multiple_of(n * pair, LANES), pair)
-
-        def core_copy(n):
-            return remote(
-                core_out.at[k, :, :, at(n)], core_in.at[k, :, :, at(n)],
-                core_send.at[k, n], core_recv.at[k, n], {"pix": z * CORES + other},
-            )
-
-        def tile(side, n):
-            out = None
-            for left, right in pairs:
-                term = dot_rows(
-                    frames_s[left, :, side].reshape(n_z * piece, half),
-                    frames_s[right, n].reshape(pair, half),
-                )
-                out = term if out is None else out + term
-            return out.reshape(n_z, piece, pair)
-
-        @pl.loop(0, n_z)
-        def _(n):
-            core_out[k, :, :, at(n)] = tile(other, n)
-            core_copy(n).start()
-
-        @pl.loop(0, n_z)
-        def _(n):
-            value = tile(core, n)
-            core_copy(n).wait()
-            value = value + core_in[k, :, :, at(n)]
-            value = value * widened(cols[row_block, 1, :, core], pair)
-            acc[k, :, :, at(n)] = value * rows[col_block, 0:1, at(n)]
-
-    def z_base(s):
-        return n_z - (n_z >> s)
-
-    def z_copy(k, s, m):
+        for n in range(n_z):
+            multiply_columns(k, pairs, n)
+        for n in range(n_z):
+            merge_columns(k, n, row_block, col_block)
+
+    def z_copy(k, s, m, part, c):
         bit = 1 << s
         sign = 1 - 2 * lax.rem(z // bit, 2)
-        at = z_base(s) + m
+        at = n_z - (n_z >> s) + m
         return remote(
-            z_out.at[k, at], z_in.at[k, at], z_send.at[k, at], z_recv.at[k, at],
+            z_out.at[k, at, :, part], z_in.at[k, at, :, part], z_send.at[k, at, c], z_recv.at[k, at, c],
             {"pix": (z + sign * bit) * CORES + core},
         )
 
-    def z_send_stage(k, s):
+    def z_put(k, s, m, part=everything, c=0):
         bit = 1 << s
-        low, top = lax.rem(z, bit), lax.rem(z // bit, 2)
-        for m in range(n_z >> (s + 1)):
-            j = m * 2 * bit + (1 - top) * bit + low
-            z_out[k, z_base(s) + m] = quantized(acc[k, j])
-            z_copy(k, s, m).start()
-
-    def z_recv_stage(k, s):
+        j = m * 2 * bit + (1 - lax.rem(z // bit, 2)) * bit + lax.rem(z, bit)
+        z_out[k, n_z - (n_z >> s) + m, :, part] = quantized(prod[k, j, core, :, part])
+        z_copy(k, s, m, part, c).start()
+
+    def z_get(k, s, m, part=everything, c=0, both=True):
         bit = 1 << s
-        for m in range(n_z >> (s + 1)):
-            z_copy(k, s, m).wait()
-            j = m * 2 * bit + lax.rem(z, 2 * bit)
-            acc[k, j] = acc[k, j] + restored(z_in[k, z_base(s) + m])
-
+        copy = z_copy(k, s, m, part, c)
+        copy.wait_recv()
+        if both:
+            copy.wait_send()
+        j = m * 2 * bit + lax.rem(z, 2 * bit)
+        prod[k, j, core, :, part] = prod[k, j, core, :, part] + restored(z_in[k, n_z - (n_z >> s) + m, :, part])
+
+    def order(s):
+        count = n_z >> (s + 1)
+        if count == 1:
+            return [0], []
+        held = lax.rem(z // (2 << s), 2)
+        return [2 * i + 1 - held for i in range(count // 2)], [2 * i + held for i in range(count // 2)]
+
+    def advance(k, s, part=everything, c=0):
+        ahead, after = order(s) if s >= 0 else ((), ())
+        for m in ahead:
+            z_get(k, s, m, part, c)
+        if s + 1 < stages:
+            for m in sum(order(s + 1), []):
+                z_put(k, s + 1, m, part, c)
+        for m in after:
+            z_get(k, s, m, part, c)
+
+    def at_stage(s, j, sends):
+        bit = 1 << s
+        same = lax.rem(z // bit, 2) == (j >> s) % 2
+        return jnp.logical_and(lax.rem(z, bit) == j % bit, jnp.logical_not(same) if sends else same)
+
+    def advance_rows(k, s, j):
+        if s >= 0:
+            @pl.when(at_stage(s, j, False))
+            def _():
+                z_get(k, s, j >> (s + 1), both=False)
+        if s + 1 < stages:
+            @pl.when(at_stage(s + 1, j, True))
+            def _():
+                z_put(k, s + 1, j >> (s + 2))
+
+    def finish_diag():
+        advance(0, stages - 1)
+        diag_ref[...] = prod[0, z, core] * widened(cols[me, 2, z, core], n_rows) * (rows[me, 1:2, :] * inverse_total)
+
+    def receive(q):
+        for slot, which, target, _, arrives in streams:
+            @pl.when(arrives)
+            def _(slot=slot, which=which, target=target):
+                data(slot, which, target, q).wait_recv()
+                source = (across if slot == 0 else up) if square else 1
+                scale_frames(frames_s, 2 + slot, 2 + slot, (x if square else slot) * half, q, source)
+
+    inverse_total = 1.0 / jnp.full((1, 1), pixel_total, F32)
     product(0, ((0, 0), (1, 1)), me, me)
-    for s in range(stages):
-        z_send_stage(0, s)
-        z_recv_stage(0, s)
-    inverse_total = 1.0 / jnp.full((1, 1), pixel_total, F32)
-    diag_ref[...] = acc[0, z] * widened(cols[me, 2, z, core], n_rows) * (rows[me, 1:2, :] * inverse_total)
+    advance(0, -1)
 
     if square:
         for d in range(1, 4):
@@ -298,66 +350,103 @@
             tot_next().wait_recv()
             take(1)
 
-    for q in range(n_z):
-        for slot, which, target, _, arrives in streams:
-            @pl.when(arrives)
-            def _(slot=slot, which=which, target=target):
-                data(slot, which, target, q).wait_recv()
-                source = (across if slot == 0 else up) if square else 1
-                scale_frames(frames_s, 2 + slot, 2 + slot, (x if square else slot) * half, q, source)
-
     if square:
-        later, sooner = jnp.maximum(block, across), jnp.minimum(block, across)
-        product(1, ((jnp.where(x == 0, 2, 1), jnp.where(x == 0, 0, 2)),), later, sooner)
-
-        @pl.when(outer)
-        def _():
-            product(2, ((jnp.where(x == 0, 3, 2), jnp.where(x == 0, 2, 3)),), 2, 1)
-
-        for s in range(stages):
-            z_send_stage(1, s)
-
-            @pl.when(outer)
-            def _():
-                z_send_stage(2, s)
-
-            z_recv_stage(1, s)
-
-            @pl.when(outer)
-            def _():
-                z_recv_stage(2, s)
-
         even = x == 0
+        odd = x == 1
 
         def last(source, slot, target):
             return remote(last_out.at[source], last_in.at[slot], last_send.at[source], last_recv.at[slot], {"frames": target})
 
+        def onward(q, s):
+            @pl.when(even)
+            def _():
+                advance_rows(1, s, q)
+
+            @pl.when(odd)
+            def _():
+                advance(1, s, lanes_of(q), q)
+
+        for q in range(n_z):
+            receive(q)
+
+            @pl.when(even)
+            def _():
+                multiply_rows(1, 2, 0, q)
+
+            @pl.when(odd)
+            def _():
+                multiply_columns(1, ((1, 2),), q)
+
+            if q == n_z - 1:
+                @pl.when(outer)
+                def _():
+                    for n in range(n_z):
+                        multiply_columns(2, ((jnp.where(even, 3, 2), jnp.where(even, 2, 3)),), n)
+
+            @pl.when(even)
+            def _():
+                merge_rows(1, q, across, block)
+
+            @pl.when(odd)
+            def _():
+                merge_columns(1, q, block, across)
+
+            onward(q, -1)
+            for s in range(stages):
+                if s < q:
+                    onward(q - 1 - s, s)
+            if q < stages - 1:
+                advance(0, q)
+
+        @pl.when(outer)
+        def _():
+            for n in range(n_z):
+                merge_columns(2, n, 2, 1)
+            advance(2, -1)
+
+        remaining = [(q, s) for q in range(n_z) for s in range(max(n_z - 1 - q, 0), stages)]
+        for q, s in remaining[:-1]:
+            onward(q, s)
+
+        @pl.when(outer)
+        def _():
+            for s in range(stages - 1):
+                advance(2, s)
+
+        for q, s in remaining[-1:]:
+            onward(q, s)
+
         @pl.when(even)
         def _():
-            last_out[0] = quantized(acc[1, z])
+            last_out[0] = quantized(prod[1, z, core])
             last(0, 0, across).start()
 
+        finish_diag()
+
+        @pl.when(outer)
+        def _():
+            advance(2, stages - 1)
+            last_out[1] = quantized(prod[2, z, core])
+
         @pl.when(block == 0)
         def _():
-            last_out[1] = quantized(acc[2, z])
             last(1, 1, up).start()
 
         @pl.when(block == 3)
         def _():
-            last_out[1] = quantized(acc[2, z])
             last(1, 0, across).start()
-
-        @pl.when(block == 0)
-        def _():
-            off_ref[...] = jnp.zeros_like(off_ref)
 
         def write(value):
             off_ref[...] = value * widened(cols[block, 2, z, core], n_rows) * (rows[before, 1:2, :] * inverse_total)
 
-        @pl.when(x == 1)
+        @pl.when(block == 0)
+        def _():
+            off_ref[...] = jnp.zeros_like(off_ref)
+
+        @pl.when(odd)
         def _():
             last(0, 0, across).wait_recv()
-            write(acc[1, z] + restored(last_in[0]))
+            write(prod[1, z, core] + restored(last_in[0]))
 
         @pl.when(block == 2)
         def _():
@@ -368,22 +457,33 @@
         @pl.when(even)
         def _():
             last(0, 0, across).wait_send()
+            for s in range(stages):
+                for j in range(n_z):
+                    @pl.when(at_stage(s, j, True))
+                    def _(s=s, j=j):
+                        z_copy(1, s, j >> (s + 1), everything, 0).wait_send()
 
         @pl.when(outer)
         def _():
             last(1, 1, up).wait_send()
     else:
+        for s in range(stages - 1):
+            advance(0, s)
+        for q in range(n_z):
+            receive(q)
+
         @pl.when(has_prev)
         def _():
             product(1, ((0, 2), (1, 3)), 0, 1)
-            for s in range(stages):
-                z_send_stage(1, s)
-                z_recv_stage(1, s)
-            off_ref[...] = acc[1, z] * widened(cols[0, 2, z, core], n_rows) * (rows[1, 1:2, :] * inverse_total)
+            for s in range(-1, stages):
+                advance(1, s)
+            off_ref[...] = prod[1, z, core] * widened(cols[0, 2, z, core], n_rows) * (rows[1, 1:2, :] * inverse_total)
 
         @pl.when(jnp.logical_not(has_prev))
         def _():
             off_ref[...] = jnp.zeros_like(off_ref)
+
+        finish_diag()
 
     for d in range(1, n_pix):
         stat(d).wait_send()
@@ -428,8 +528,7 @@
             pltpu.VMEM((blocks, 8, n_rows), F32),
             pltpu.VMEM((blocks, 8, n_rows), F32),
             pltpu.VMEM((blocks, 3, n_z, CORES, piece, LANES), F32),
-            pltpu.VMEM((tiles, n_z, piece, n_rows), F32),
-            pltpu.VMEM((tiles, n_z, piece, n_rows), F32),
+            pltpu.VMEM((tiles, n_z, CORES, piece, n_rows), F32),
             pltpu.VMEM((tiles, n_z, piece, n_rows), F32),
             pltpu.VMEM((tiles, sent, piece, n_rows), jnp.int16),
             pltpu.VMEM((tiles, sent, piece, n_rows), jnp.int16),
@@ -440,7 +539,7 @@
             dma((n_pix,)), dma((n_pix,)),
             dma((4,)), dma((4,)),
             dma((tiles, n_z)), dma((tiles, n_z)),
-            dma((tiles, sent)), dma((tiles, sent)),
+            dma((tiles, sent, n_z)), dma((tiles, sent, n_z)),
             dma((2,)), dma((2,)),
         ],
         compiler_params=pltpu.CompilerParams(

time: 128 us -> 127 us (level)
    pallas_call x1, Pallas kernels: 123 us -> 122 us  [on_device(): pl.pallas_call(functools.partial(kernel, n_frames, n_pix), out_shape=(out...]
where the time goes in v4:
time: 127 us; the launch traced here: 126 us
  Pallas kernels  122 us (96%)
  local copies, waits for them, and re-layouts  3.77 us (3%)
    pallas_call x1, Pallas kernels, on_device(): pl.pallas_call(functools.partial(kernel, n_frames, n_pix), out_shape=(out...  122 us
    unnamed x2, local copies, waits for them, and re-layouts  3.77 us

profile of v4, /device:TPU:0, one launch (start us, length us, event | category | flops | bytes accessed | tf_op | source)
XLA Modules:
  0.0 126.3 jit_solution(4553284237444179509)
XLA Ops:
  0.6 121.9 %shard_map.50 = (f32[128,1024]{1,0:T(8,128)}, f32[128,1024]{1,0:T(8,128)}) custom-call(s32[8]{0:T(128)} %owner_ref.1, s32[1024,2048]{1,0:T(8,128)} %counts_hbm.1, f32[1,2048]{1,0:T(1,128)} %bitcast.1), custom_call_target="tpu_custom_call" | custom-call | flops 8589934592 | bytes 8388608 | tf_op jit(solution)/shard_map/pallas_call | solution.py:512
  122.6 1.9 %copy.7 = f32[128,1024]{1,0:T(8,128)} copy(f32[128,1024]{1,0:T(8,128)} %get-tuple-element.4) | data formatting | bytes 1048576
  124.4 1.9 %copy.8 = f32[128,1024]{1,0:T(8,128)} copy(f32[128,1024]{1,0:T(8,128)} %get-tuple-element.5) | data formatting | bytes 1048576

commit v5 on v4

--- a/solution.py
+++ b/solution.py
@@ -126,7 +126,9 @@
 
     stats[pix] = jnp.zeros((8, n_rows), F32)
     small = 16
-    for q in range(n_z):
+    band = min(piece, 32)
+    @pl.loop(0, n_z)
+    def _(q):
         load(q).wait()
 
         @pl.loop(0, piece // small)
@@ -141,14 +143,15 @@
             def _(slot=slot, which=which, target=target):
                 data(slot, which, target, q).start()
 
-    for q in range(n_z):
+    @pl.loop(0, n_z)
+    def _(q):
         sums = jnp.zeros((pair, LANES), F32)
         for h in range(2):
             held = own[h, q].reshape(pair, half)
             lanes = slice(h * half, (h + 1) * half)
             sums = sums + dot_rows(held, sum_rows[0, :, lanes]) + dot_rows(held * held, sum_rows[1, :, lanes])
         sums = jnp.transpose(sums)
-        part = slice(q * pair, (q + 1) * pair)
+        part = pl.ds(pl.multiple_of(q * pair, LANES), pair)
         stats[pix, 0:1, part] = sums[0:1] + sums[1:2] + sums[2:3]
         stats[pix, 1:2, part] = sums[3:4]
 
@@ -222,7 +225,12 @@
     everything = slice(None)
 
     def lanes_of(n):
-        return pl.ds(n * pair, pair)
+        return pl.ds(pl.multiple_of(n * pair, LANES), pair)
+
+    def by_rows(body):
+        @pl.loop(0, piece // band)
+        def _(i):
+            body(pl.ds(pl.multiple_of(i * band, band), band))
 
     def core_columns(k, n):
         return remote(
@@ -246,25 +254,40 @@
 
     def merge_columns(k, n, row_block, col_block):
         core_columns(k, n).wait()
-        value = prod[k, :, core, :, lanes_of(n)] + core_in[k, :, :, lanes_of(n)]
-        value = value * widened(cols[row_block, 1, :, core], pair)
-        prod[k, :, core, :, lanes_of(n)] = value * rows[col_block, 0:1, lanes_of(n)]
+
+        @pl.loop(0, n_z)
+        def _(j):
+            def body(at):
+                value = prod[k, j, core, at, lanes_of(n)] + core_in[k, j, at, lanes_of(n)]
+                value = value * widened(cols[row_block, 1, j, core, at, :], pair)
+                prod[k, j, core, at, lanes_of(n)] = value * rows[col_block, 0:1, lanes_of(n)]
+
+            by_rows(body)
 
     def multiply_rows(k, left, right, j):
-        for n in range(n_z):
+        @pl.loop(0, n_z)
+        def _(n):
             out = dot_rows(frames_s[left, j].reshape(pair, half), frames_s[right, n].reshape(pair, half))
             prod[k, j, :, :, lanes_of(n)] = out.reshape(CORES, piece, pair)
+
         core_rows(k, j).start()
 
     def merge_rows(k, j, row_block, col_block):
         core_rows(k, j).wait()
-        value = (prod[k, j, core] + core_in[k, j]) * widened(cols[row_block, 1, j, core], n_rows)
-        prod[k, j, core] = value * rows[col_block, 0:1, :]
+
+        def body(at):
+            value = (prod[k, j, core, at, :] + core_in[k, j, at, :]) * widened(cols[row_block, 1, j, core, at, :], n_rows)
+            prod[k, j, core, at, :] = value * rows[col_block, 0:1, :]
+
+        by_rows(body)
 
     def product(k, pairs, row_block, col_block):
-        for n in range(n_z):
+        @pl.loop(0, n_z)
+        def _(n):
             multiply_columns(k, pairs, n)
-        for n in range(n_z):
+
+        @pl.loop(0, n_z)
+        def _(n):
             merge_columns(k, n, row_block, col_block)
 
     def z_copy(k, s, m, part, c):
@@ -279,7 +302,11 @@
     def z_put(k, s, m, part=everything, c=0):
         bit = 1 << s
         j = m * 2 * bit + (1 - lax.rem(z // bit, 2)) * bit + lax.rem(z, bit)
-        z_out[k, n_z - (n_z >> s) + m, :, part] = quantized(prod[k, j, core, :, part])
+
+        def body(at):
+            z_out[k, n_z - (n_z >> s) + m, at, part] = quantized(prod[k, j, core, at, part])
+
+        by_rows(body)
         z_copy(k, s, m, part, c).start()
 
     def z_get(k, s, m, part=everything, c=0, both=True):
@@ -289,7 +316,12 @@
         if both:
             copy.wait_send()
         j = m * 2 * bit + lax.rem(z, 2 * bit)
-        prod[k, j, core, :, part] = prod[k, j, core, :, part] + restored(z_in[k, n_z - (n_z >> s) + m, :, part])
+
+        def body(at):
+            came = restored(z_in[k, n_z - (n_z >> s) + m, at, part])
+            prod[k, j, core, at, part] = prod[k, j, core, at, part] + came
+
+        by_rows(body)
 
     def order(s):
         count = n_z >> (s + 1)
@@ -309,23 +341,28 @@
             z_get(k, s, m, part, c)
 
     def at_stage(s, j, sends):
-        bit = 1 << s
-        same = lax.rem(z // bit, 2) == (j >> s) % 2
-        return jnp.logical_and(lax.rem(z, bit) == j % bit, jnp.logical_not(same) if sends else same)
+        bit, j = 1 << s, jnp.int32(j)
+        same = lax.rem(z // bit, 2) == lax.rem(j // bit, 2)
+        return jnp.logical_and(lax.rem(z, bit) == lax.rem(j, bit), jnp.logical_not(same) if sends else same)
 
     def advance_rows(k, s, j):
         if s >= 0:
             @pl.when(at_stage(s, j, False))
             def _():
-                z_get(k, s, j >> (s + 1), both=False)
+                z_get(k, s, j // (2 << s), both=False)
         if s + 1 < stages:
             @pl.when(at_stage(s + 1, j, True))
             def _():
-                z_put(k, s + 1, j >> (s + 2))
+                z_put(k, s + 1, j // (2 << (s + 1)))
 
     def finish_diag():
         advance(0, stages - 1)
-        diag_ref[...] = prod[0, z, core] * widened(cols[me, 2, z, core], n_rows) * (rows[me, 1:2, :] * inverse_total)
+
+        def body(at):
+            value = prod[0, z, core, at, :] * widened(cols[me, 2, z, core, at, :], n_rows)
+            diag_ref[at, :] = value * (rows[me, 1:2, :] * inverse_total)
+
+        by_rows(body)
 
     def receive(q):
         for slot, which, target, _, arrives in streams:
@@ -342,7 +379,9 @@
     if square:
         for d in range(1, 4):
             tot_from(d).wait_recv()
-        for d in range(1, 4):
+
+        @pl.loop(1, 4)
+        def _(d):
             take(lax.rem(block + d, 4))
     else:
         @pl.when(has_prev)
@@ -356,6 +395,12 @@
 
         def last(source, slot, target):
             return remote(last_out.at[source], last_in.at[slot], last_send.at[source], last_recv.at[slot], {"frames": target})
+
+        def pack(slot, k):
+            def body(at):
+                last_out[slot, at, :] = quantized(prod[k, z, core, at, :])
+
+            by_rows(body)
 
         def onward(q, s):
             @pl.when(even)
@@ -366,42 +411,34 @@
             def _():
                 advance(1, s, lanes_of(q), q)
 
-        for q in range(n_z):
+        @pl.loop(0, n_z)
+        def _(q):
             receive(q)
 
             @pl.when(even)
             def _():
                 multiply_rows(1, 2, 0, q)
+                merge_rows(1, q, across, block)
 
             @pl.when(odd)
             def _():
                 multiply_columns(1, ((1, 2),), q)
-
-            if q == n_z - 1:
-                @pl.when(outer)
-                def _():
-                    for n in range(n_z):
-                        multiply_columns(2, ((jnp.where(even, 3, 2), jnp.where(even, 2, 3)),), n)
-
-            @pl.when(even)
-            def _():
-                merge_rows(1, q, across, block)
-
-            @pl.when(odd)
-            def _():
                 merge_columns(1, q, block, across)
 
             onward(q, -1)
             for s in range(stages):
-                if s < q:
+                @pl.when(q > s)
+                def _(s=s):
                     onward(q - 1 - s, s)
-            if q < stages - 1:
-                advance(0, q)
+
+            @pl.when(q == 0)
+            def _():
+                for s in range(stages - 1):
+                    advance(0, s)
 
         @pl.when(outer)
         def _():
-            for n in range(n_z):
-                merge_columns(2, n, 2, 1)
+            product(2, ((jnp.where(even, 3, 2), jnp.where(even, 2, 3)),), 2, 1)
             advance(2, -1)
 
         remaining = [(q, s) for q in range(n_z) for s in range(max(n_z - 1 - q, 0), stages)]
@@ -418,7 +455,7 @@
 
         @pl.when(even)
         def _():
-            last_out[0] = quantized(prod[1, z, core])
+            pack(0, 1)
             last(0, 0, across).start()
 
         finish_diag()
@@ -426,7 +463,7 @@
         @pl.when(outer)
         def _():
             advance(2, stages - 1)
-            last_out[1] = quantized(prod[2, z, core])
+            pack(1, 2)
 
         @pl.when(block == 0)
         def _():
@@ -437,7 +474,11 @@
             last(1, 0, across).start()
 
         def write(value):
-            off_ref[...] = value * widened(cols[block, 2, z, core], n_rows) * (rows[before, 1:2, :] * inverse_total)
+            def body(at):
+                scale = widened(cols[block, 2, z, core, at, :], n_rows)
+                off_ref[at, :] = value(at) * scale * (rows[before, 1:2, :] * inverse_total)
+
+            by_rows(body)
 
         @pl.when(block == 0)
         def _():
@@ -446,22 +487,24 @@
         @pl.when(odd)
         def _():
             last(0, 0, across).wait_recv()
-            write(prod[1, z, core] + restored(last_in[0]))
+            write(lambda at: prod[1, z, core, at, :] + restored(last_in[0, at, :]))
 
         @pl.when(block == 2)
         def _():
             last(0, 0, across).wait_recv()
             last(1, 1, up).wait_recv()
-            write(restored(last_in[0]) + restored(last_in[1]))
+            write(lambda at: restored(last_in[0, at, :]) + restored(last_in[1, at, :]))
 
         @pl.when(even)
         def _():
             last(0, 0, across).wait_send()
-            for s in range(stages):
-                for j in range(n_z):
+
+            @pl.loop(0, n_z)
+            def _(j):
+                for s in range(stages):
                     @pl.when(at_stage(s, j, True))
-                    def _(s=s, j=j):
-                        z_copy(1, s, j >> (s + 1), everything, 0).wait_send()
+                    def _(s=s):
+                        z_copy(1, s, j // (2 << s), everything, 0).wait_send()
 
         @pl.when(outer)
         def _():

time: 127 us -> 126 us (level)
  no operation moved by 1% of the time
where the time goes in v5:
time: 126 us; the launch traced here: 125 us
  Pallas kernels  121 us (96%)
  local copies, waits for them, and re-layouts  3.77 us (3%)
    pallas_call x1, Pallas kernels, on_device(): pl.pallas_call(functools.partial(kernel, n_frames, n_pix), out_shape=(out...  121 us
    unnamed x2, local copies, waits for them, and re-layouts  3.77 us

profile of v5, /device:TPU:0, one launch (start us, length us, event | category | flops | bytes accessed | tf_op | source)
XLA Modules:
  0.0 125.3 jit_solution(2768249054450111135)
XLA Ops:
  0.6 120.9 %shard_map.50 = (f32[128,1024]{1,0:T(8,128)}, f32[128,1024]{1,0:T(8,128)}) custom-call(s32[8]{0:T(128)} %owner_ref.1, s32[1024,2048]{1,0:T(8,128)} %counts_hbm.1, f32[1,2048]{1,0:T(1,128)} %bitcast.1), custom_call_target="tpu_custom_call" | custom-call | flops 8589934592 | bytes 8388608 | tf_op jit(solution)/shard_map/pallas_call | solution.py:555
  121.5 1.9 %copy.7 = f32[128,1024]{1,0:T(8,128)} copy(f32[128,1024]{1,0:T(8,128)} %get-tuple-element.4) | data formatting | bytes 1048576
  123.4 1.9 %copy.8 = f32[128,1024]{1,0:T(8,128)} copy(f32[128,1024]{1,0:T(8,128)} %get-tuple-element.5) | data formatting | bytes 1048576

commit v6 on v3

--- a/solution.py
+++ b/solution.py
@@ -238,20 +238,19 @@
                     frames_s[right, n].reshape(pair, half),
                 )
                 out = term if out is None else out + term
-            return out.reshape(n_z, piece, pair)
+            out = out.reshape(n_z, piece, pair) * widened(cols[row_block, 1, :, side], pair)
+            return out * rows[col_block, 0:1, at(n)]
 
         @pl.loop(0, n_z)
         def _(n):
-            core_out[k, :, :, at(n)] = tile(other, n)
+            core_out[k, :, :, at(n)] = quantized(tile(other, n))
             core_copy(n).start()
 
         @pl.loop(0, n_z)
         def _(n):
             value = tile(core, n)
             core_copy(n).wait()
-            value = value + core_in[k, :, :, at(n)]
-            value = value * widened(cols[row_block, 1, :, core], pair)
-            acc[k, :, :, at(n)] = value * rows[col_block, 0:1, at(n)]
+            acc[k, :, :, at(n)] = value + restored(core_in[k, :, :, at(n)])
 
     def z_base(s):
         return n_z - (n_z >> s)
@@ -450,8 +449,8 @@
             pltpu.VMEM((blocks, 8, n_rows), F32),
             pltpu.VMEM((blocks, 8, n_rows), F32),
             pltpu.VMEM((blocks, 3, n_z, CORES, piece, LANES), F32),
-            pltpu.VMEM((tiles, n_z, piece, n_rows), F32),
-            pltpu.VMEM((tiles, n_z, piece, n_rows), F32),
+            pltpu.VMEM((tiles, n_z, piece, n_rows), jnp.int16),
+            pltpu.VMEM((tiles, n_z, piece, n_rows), jnp.int16),
             pltpu.VMEM((tiles, n_z, piece, n_rows), F32),
             pltpu.VMEM((tiles, sent, piece, n_rows), jnp.int16),
             pltpu.VMEM((tiles, sent, piece, n_rows), jnp.int16),

time: 121 us -> 120 us (level)
  the two profiles are of different devices: /device:TPU:0 before, /device:TPU:28 now
where the time goes in v6:
time: 120 us
  Pallas kernels  116 us (97%)
  local copies, waits for them, and re-layouts  3.77 us (3%)
    pallas_call x1, Pallas kernels, on_device(): pl.pallas_call(functools.partial(kernel, n_frames, n_pix), out_shape=(out...  116 us
    unnamed x2, local copies, waits for them, and re-layouts  3.77 us

profile of v6, /device:TPU:28, one launch (start us, length us, event | category | flops | bytes accessed | tf_op | source)
XLA Modules:
  0.0 120.0 jit_solution(7169720234013046896)
XLA Ops:
  0.6 115.6 %shard_map.50 = (f32[128,1024]{1,0:T(8,128)}, f32[128,1024]{1,0:T(8,128)}) custom-call(s32[8]{0:T(128)} %owner_ref.1, s32[1024,2048]{1,0:T(8,128)} %counts_hbm.1, f32[1,2048]{1,0:T(1,128)} %bitcast.1), custom_call_target="tpu_custom_call" | custom-call | flops 8589934592 | bytes 8388608 | tf_op jit(solution)/shard_map/pallas_call | solution.py:433
  116.3 1.9 %copy.7 = f32[128,1024]{1,0:T(8,128)} copy(f32[128,1024]{1,0:T(8,128)} %get-tuple-element.4) | data formatting | bytes 1048576
  118.1 1.9 %copy.8 = f32[128,1024]{1,0:T(8,128)} copy(f32[128,1024]{1,0:T(8,128)} %get-tuple-element.5) | data formatting | bytes 1048576
